TPU v7x, 256 devices: a whole 4x4x8 slice. The times are simulated.
256 devices in a mesh: ctx: 128 (over z, y_lo, x, core), grp: 2 (over y_hi).
Axes of the slice: x: 4, y: 4 (y_hi: 2, y_lo: 2; y = y_hi * 2 + y_lo), z: 8, core: 2. Of those that a mesh axis runs over, the one named last changes fastest.
Arguments:
- queries: bfloat16 [24576, 1024], P('ctx', 'grp'), may hold values from -80 to 80
- keys: bfloat16 [24576, 128], P('ctx'), may hold values from -4 to 4
- values: bfloat16 [24576, 128], P('ctx'), may hold values from -6 to 6
- span_order: int32 [256], P('ctx'), may hold values from 0 to 255, each once
- w_out: bfloat16 [1024, 5120], P('grp'), may hold values from -0.1875 to 0.1875
Outputs:
- projected: bfloat16 [24576, 5120], P('ctx', 'grp')
Inputs may be any that keep to these rules, and one draw needn't show every extreme that they name: `span_order`: a permutation: each block of positions is held by exactly one stored block.
All inputs are finite; a program needn't handle non-finite values.
Results may differ from a plain program's by a relative error of at most 0.015.
Values may be sent and summed in bfloat16 or wider, within the bound.
A program may use at most 128 MiB of HBM per device.

v0:
```python
import math

import jax
import jax.numpy as jnp
from jax import lax
from jax.sharding import PartitionSpec as P

HD = 128


def global_positions(order_table, start, count, span):
    row_ids = start + jnp.arange(count, dtype=jnp.int32)
    return order_table[row_ids // span] * span + row_ids % span


def absorb(state, query_heads, query_pos, key_block, value_block, key_pos):
    accumulated, running_max, denominator = state
    scores = jnp.einsum(
        "hrd,cd->hrc", query_heads, key_block, preferred_element_type=jnp.float32
    ) * HD ** (-0.5)
    visible = key_pos[None, None, :] <= query_pos[None, :, None]
    scores = jnp.where(visible, scores, -1e30)
    new_max = jnp.maximum(running_max, jnp.max(scores, axis=-1))
    fade_factor = jnp.exp(running_max - new_max)
    weights = jnp.where(visible, jnp.exp(scores - new_max[:, :, None]), 0.0)
    denominator = denominator * fade_factor + jnp.sum(weights, axis=-1)
    update = jnp.einsum(
        "hrc,cd->hrd", weights.astype(jnp.bfloat16), value_block, preferred_element_type=jnp.float32
    )
    accumulated = accumulated * fade_factor[:, :, None] + update
    return (accumulated, new_max, denominator)


def sweep_keys(state, query_heads, query_pos, key_rows, value_rows, key_pos):
    count = key_rows.shape[0]
    block_rows = math.gcd(count, 512)
    steps_count = count // block_rows

    def step_block(carry, pieces):
        return (absorb(carry, query_heads, query_pos, pieces[0], pieces[1], pieces[2]), None)

    stacked = (
        key_rows.reshape(steps_count, block_rows, -1),
        value_rows.reshape(steps_count, block_rows, -1),
        key_pos.reshape(steps_count, block_rows),
    )
    state, unused = lax.scan(step_block, state, stacked)
    return state


def body(queries, keys, values, span_order, w_out):
    row_count = queries.shape[0]
    head_count = queries.shape[1] // HD
    span = row_count // 2
    order_table = lax.all_gather(span_order, "ctx", axis=0, tiled=True)
    shard_index = lax.axis_index("ctx")
    query_pos = global_positions(order_table, shard_index * row_count, row_count, span)
    query_heads = jnp.transpose(queries.reshape(row_count, head_count, HD), (1, 0, 2))
    initial = (
        jnp.zeros((head_count, row_count, HD), jnp.float32),
        jnp.full((head_count, row_count), -1e30, jnp.float32),
        jnp.zeros((head_count, row_count), jnp.float32),
    )
    pieces = (
        lax.all_gather(keys, "ctx", axis=0, tiled=True),
        lax.all_gather(values, "ctx", axis=0, tiled=True),
    )
    key_pos = global_positions(order_table, jnp.int32(0), pieces[0].shape[0], span)
    state = sweep_keys(initial, query_heads, query_pos, pieces[0], pieces[1], key_pos)
    accumulated, running_max, denominator = state
    context = (accumulated / denominator[:, :, None]).astype(jnp.bfloat16)
    context = jnp.transpose(context, (1, 0, 2)).reshape(row_count, head_count * HD)
    partial_term = jnp.dot(context, w_out, preferred_element_type=jnp.float32)
    return lax.psum_scatter(
        partial_term.astype(jnp.bfloat16), "grp", scatter_dimension=1, tiled=True
    )


def solution(mesh):
    return jax.shard_map(
        body,
        mesh=mesh,
        in_specs=(P("ctx", "grp"), P("ctx", None), P("ctx", None), P("ctx"), P("grp", None)),
        out_specs=P("ctx", "grp"),
        check_vma=False,
    )
```

profile of v0, /device:TPU:1, one launch (start us, length us, event | category | flops | bytes accessed | tf_op | source)
XLA Modules:
  0.0 674.5 jit_solution(10282038666977394557)
XLA Ops:
  10.9 22.7 %all-reduce = s32[256]{0:T(256)S(1)} all-reduce(s32[256]{0:T(256)S(1)} %dynamic-update-slice), channel_id=1, replica_groups=mesh['ctx'=128,'grp'=2] {'ctx'}, use_global_device_ids=true, to_apply=%add | all-reduce | flops 256 | bytes 2048
  33.7 1.6 gather_fusion.1
  35.5 152.5 %gather_fusion = s32[24576]{0:T(1024)S(1)} fusion(s32[256]{0:T(256)S(1)} %all-reduce, s32[24576]{0:T(1024)S(1)} %broadcast_clamp_fusion), kind=kCustom, calls=%fused_computation | custom fusion | bytes 294912 | tf_op jit(solution)/shard_map/gather | solution.py:13
  188.3 42.9 %all-gather.3.cloned.1.call-done = bf16[24576,128]{1,0:T(8,128)(2,1)} async-done(((bf16[192,128]{1,0:T(8,128)(2,1)}), bf16[24576,128]{1,0:T(8,128)(2,1)}) %all-gather.3.cloned.1.call-update) | async-done | bytes 6291472 | tf_op jit(solution)/shard_map/all_gather | solution.py:65
  231.2 219.2 %all-gather.5.cloned.1.call-done = bf16[24576,128]{1,0:T(8,128)(2,1)} async-done(((bf16[192,128]{1,0:T(8,128)(2,1)}), bf16[24576,128]{1,0:T(8,128)(2,1)}) %all-gather.5.cloned.1.call-update) | async-done | bytes 6291472 | tf_op jit(solution)/shard_map/all_gather | solution.py:66
  450.5 175.4 %while.15 = (s32[]{:T(128)}, f32[4,192,128]{2,1,0:T(8,128)S(1)}, f32[4,192]{1,0:T(4,128)S(1)}, f32[4,192]{1,0:T(4,128)S(1)}, s32[48,512]{1,0:T(8,128)S(1)}, /*in...) while((s32[]{:T(128)}, f32[4,192,128]{2,1,0:T(8,128)S(1)}, ...), condition=%wide.region_3.4_spmd.clone, body=%wide.region_0.3_spmd.clone.sunk | while | flops 205262592 | bytes 6414205 | solution.py:47
  452.6 1.5 convolution_add_fusion.2
  456.3 1.5 convolution_add_fusion.2
  459.9 1.5 convolution_add_fusion.2
  474.6 1.5 convolution_add_fusion.2
  478.2 1.5 convolution_add_fusion.2
  481.9 1.5 convolution_add_fusion.2
  496.5 1.5 convolution_add_fusion.2
  500.1 1.5 convolution_add_fusion.2
  503.8 1.5 convolution_add_fusion.2
  507.4 1.5 convolution_add_fusion.2
  518.4 1.5 convolution_add_fusion.2
  522.1 1.5 convolution_add_fusion.2
  525.7 1.5 convolution_add_fusion.2
  529.4 1.5 convolution_add_fusion.2
  544.0 1.5 convolution_add_fusion.2
  547.6 1.5 convolution_add_fusion.2
  551.3 1.5 convolution_add_fusion.2
  565.9 1.5 convolution_add_fusion.2
  569.6 1.5 convolution_add_fusion.2
  573.2 1.5 convolution_add_fusion.2
  576.9 1.5 convolution_add_fusion.2
  587.8 1.5 convolution_add_fusion.2
  591.5 1.5 convolution_add_fusion.2
  595.2 1.5 convolution_add_fusion.2
  625.9 5.0 convolution_convert_fusion
  630.9 37.1 %reduce-scatter.2.cloned.1.call-done = bf16[192,2560]{1,0:T(8,128)(2,1)} async-done(((bf16[192,5120]{1,0:T(8,128)(2,1)}), bf16[192,2560]{1,0:T(8,128)(2,1)}) %reduce-scatter.2.cloned.1.call-update) | async-done | bytes 983056 | tf_op jit(solution)/shard_map/reduce_scatter | solution.py:74
  (384 shorter events, 141.7 us)
Async XLA Ops:
  6.5 224.7 %all-gather.3.cloned.1.call-start = ((), (), s32[]{:S(2)}) async-start(), calls=%async_computation.1 | async-start | bytes 6340608 | tf_op jit(solution)/shard_map/all_gather | solution.py:65
  7.3 443.2 %all-gather.5.cloned.1.call-start = ((), (), s32[]{:S(2)}) async-start(), calls=%async_computation.2 | async-start | bytes 6340608 | tf_op jit(solution)/shard_map/all_gather | solution.py:66
  8.0 660.0 %reduce-scatter.2.cloned.1.call-start = ((), (), s32[]{:S(2)}) async-start(), calls=%async_computation.3 | async-start | bytes 2949120 | tf_op jit(solution)/shard_map/reduce_scatter | solution.py:74
  35.5 152.6 %copy-start = (bf16[192,512]{1,0:T(8,128)(2,1)S(1)}, bf16[192,512]{1,0:T(8,128)(2,1)}, u32[]{:S(2)}) copy-start(bf16[192,512]{1,0:T(8,128)(2,1)} %param.7) | copy-start | bytes 589828
Sparse Core Ops, SparseCore 0:
  9.2 221.9 all-gather.2
  233.1 217.3 all-gather.4
  631.1 36.8 reduce-scatter.1
where the time goes:
time: 676 us; the launch traced here: 675 us
  waiting for transfers between devices  301 us (45%)
  local copies, waits for them, and re-layouts  157 us (23%)
  matrix products  143 us (21%)
  other arithmetic  34.5 us (5%)
  blocking collectives  22.7 us (3%)
  between operations  13.9 us (2%)
    all_gather x1, waiting for transfers between devices, body(): lax.all_gather(values, 'ctx', axis=0, tiled=True)  219 us
    gather x2, local copies, waits for them, and re-layouts, global_positions(): return order_table[row_ids // span] * span + row_ids % span  154 us
    dot_general x48, matrix products, absorb(): jnp.einsum('hrc,cd->hrd', weights.astype(jnp.bfloat16), value_block, pref...  70.2 us
    dot_general x48, matrix products, absorb(): jnp.einsum('hrd,cd->hrc', query_heads, key_block, preferred_element_type=...  67.7 us
    all_gather x1, waiting for transfers between devices, body(): lax.all_gather(keys, 'ctx', axis=0, tiled=True)  42.9 us
    reduce_scatter x1, waiting for transfers between devices, body(): lax.psum_scatter(partial_term.astype(jnp.bfloat16), 'grp', scatter_dimens...  37.1 us
    reduce_sum x48, other arithmetic, absorb(): denominator = denominator * fade_factor + jnp.sum(weights, axis=-1)  27.2 us
    unnamed x1, blocking collectives  22.7 us
  transfers between devices with their start and end apart: 3, of which 3 were waited for; matrix products, arithmetic and copies ran while one was open for 23% of the time, Pallas kernels for 0%

commit v1 on v0

v1 whole, which is shorter than its diff:
```python
import functools

import jax
import jax.numpy as jnp
from jax import lax
from jax.experimental import pallas as pl
from jax.experimental.pallas import tpu as pltpu
from jax.sharding import PartitionSpec as P

HD = 128
HEADS = 4
TOK = 192
SPAN = 96
HALF = 48
COLS = HEADS * TOK
TILE = 512
TILES = 4 * COLS // TILE
KEYS = 16 * HALF
BUNDLE = KEYS + 16
VROWS = 144
MESH = pl.DeviceIdType.MESH
BIG = 2.0**100
SCALE = HD**-0.5 * 1.4426950408889634
F32 = jnp.float32
BF16 = jnp.bfloat16


def iota(shape, dim):
    return lax.broadcasted_iota(jnp.int32, shape, dim)


def kernel(
    q_ref, k_ref, v_ref, order_ref, w_ref, o_ref,
    qt, pos_tx, pos_rx, stage, bundle, kaug, vt, sbuf, acc, mx, w_own, w_oth, pacc,
    p1_tx, p1_rx, s1_tx, s1_rx, p2_tx, p2_rx, s2_tx, s2_rx, c_tx, c_rx,
    one_s, one_r, q_s, q_r, pos_sem, ring_s, ring_r, w_s, w_r, w_local, tail_s, tail_r,
):
    ctx, h = lax.axis_index("ctx"), lax.axis_index("grp")
    z, ylo, x, core = ctx // 16, (ctx // 8) % 2, (ctx // 2) % 4, ctx % 2

    def device(dz=0, dy=0, dx=0, dc=0, dh=0):
        z1, x1 = (z + dz) % 8, (x + dx) % 4
        y1 = 1 - ylo if dy else ylo
        c1 = 1 - core if dc else core
        return (((z1 * 2 + y1) * 4 + x1) * 2 + c1, 1 - h if dh else h)

    def remote(src, dst, send, recv, where):
        return pltpu.make_async_remote_copy(
            src_ref=src, dst_ref=dst, send_sem=send, recv_sem=recv, device_id=where, device_id_type=MESH
        )

    plane = [(j // 4, j % 4) for j in range(1, 8)]
    mates = [(1, 0), (1, 1), (0, 1)]
    peers = [device(dy=dy, dx=dx) for dy, dx in plane] + [device(dz=dz) for dz in range(1, 8)]
    peers += [device(dc=dc, dh=dh) for dc, dh in mates] + [device(dy=1, dh=1)]
    barrier = pltpu.get_barrier_semaphore()
    for peer in peers:
        pl.semaphore_signal(barrier, inc=1, device_id=peer, device_id_type=MESH)

    def cols(group):
        return pl.ds(group * COLS, COLS)

    stacked = jnp.concatenate([q_ref[:, i * HD : (i + 1) * HD] for i in range(HEADS)], axis=0)
    qt[0:HD, cols(3)] = stacked.T
    first, second = order_ref[0].astype(F32), order_ref[1].astype(F32)
    mine = jnp.where(h == 0, first, second)
    row0 = pl.multiple_of(h * SPAN, 16)
    for route in range(2):
        rows = pl.ds(pl.multiple_of(row0 + route * HALF, 16), HALF)
        stage[route, 0, 0:HALF] = k_ref[rows, :]
        stage[route, 0, HALF : 2 * HALF] = v_ref[rows, :]
        stage[route, 0, 2 * HALF :] = jnp.full((16, HD), mine, F32).astype(BF16)
    lane = iota((16, HD), 1)
    pos_tx[...] = jnp.where(lane == 2, first, jnp.where(lane == 3, second, 0.0)).astype(BF16)

    pl.semaphore_wait(barrier, len(peers))

    one = []
    for j in range(1, 8):
        dy, dx = plane[j - 1]
        for route, where in ((0, device(dy=dy, dx=dx)), (1, device(dz=j))):
            one.append(remote(stage.at[route, 0], stage.at[route, j], one_s.at[route, j], one_r.at[route, j], where))
    swap = [
        remote(qt.at[0:HD, cols(3)], qt.at[0:HD, cols(g)], q_s.at[g], q_r.at[g], device(dc=dc, dh=dh))
        for g, (dc, dh) in enumerate(mates)
    ]
    swap.append(remote(pos_tx, pos_rx, pos_sem.at[0], pos_sem.at[1], device(dc=1)))
    for copy in one + swap:
        copy.start()

    w_half = pl.multiple_of(h * w_own.shape[1], 128)
    o_half = pl.multiple_of((1 - h) * w_own.shape[1], 128)
    w_cols = w_own.shape[1]
    his = pl.multiple_of((2 * (1 - ylo) + core) * HD, HD)
    quarter = 2 * ylo + core
    far = 2 * (1 - ylo) + core
    w_copy = pltpu.make_async_copy(w_ref.at[:, pl.ds(w_half, w_cols)], w_own, w_local)
    w_send = [
        remote(w_ref.at[pl.ds(his, HD), pl.ds(o_half, w_cols)], w_oth.at[far], w_s.at[0], w_r.at[0], device(dy=1, dh=1)),
        remote(w_oth.at[quarter], w_oth.at[quarter], w_s.at[1], w_r.at[1], device(dc=1)),
        remote(w_oth.at[quarter], w_oth.at[quarter], w_s.at[2], w_r.at[2], device(dy=1)),
        remote(w_oth.at[far], w_oth.at[far], w_s.at[3], w_r.at[3], device(dc=1)),
    ]
    w_got = [
        remote(w_oth.at[quarter], w_oth.at[quarter], w_s.at[0], w_r.at[0], device(dy=1, dh=1)),
        remote(w_oth.at[0], w_oth.at[2 * ylo + 1 - core], w_s.at[1], w_r.at[1], device(dc=1)),
        remote(w_oth.at[0], w_oth.at[far], w_s.at[2], w_r.at[2], device(dy=1)),
        remote(w_oth.at[0], w_oth.at[2 * (1 - ylo) + 1 - core], w_s.at[3], w_r.at[3], device(dc=1)),
    ]
    w_copy.start()
    w_send[0].start()

    sub = iota((HD, COLS), 0)
    col = iota((1, COLS), 1)
    token = col % TOK
    block = token // SPAN
    step_row = token % SPAN + 4
    for g in range(4):
        dc = mates[g][0] if g < 3 else 0
        hit = sub == block + 2 * dc
        if dc == 0:
            hit = jnp.logical_or(hit, jnp.logical_and(sub == step_row, block == h))
        qt[HD : 2 * HD, cols(g)] = jnp.where(hit, 1.0, 0.0).astype(BF16)
    for k in range(8):
        vt[k, HD:VROWS, :] = jnp.ones((VROWS - HD, KEYS), BF16)
    acc[...] = jnp.zeros_like(acc)
    mx[...] = jnp.full_like(mx, -BIG)

    right, left, up, down, over = device(dz=1), device(dz=7), device(dx=1), device(dx=3), device(dy=1)
    whole, front, back = pl.ds(0, BUNDLE), pl.ds(0, KEYS // 2), pl.ds(KEYS // 2, BUNDLE - KEYS // 2)
    hops = [
        (0, 0, 1, whole, right), (0, 0, 2, whole, left), (1, 0, 1, whole, up), (1, 0, 2, whole, down), (1, 0, 3, whole, over),
        (0, 1, 3, whole, right), (0, 2, 4, whole, left), (1, 3, 4, whole, up), (1, 3, 5, whole, down), (1, 1, 6, whole, up),
        (0, 3, 5, whole, right), (0, 4, 6, whole, left), (1, 5, 7, whole, down),
        (0, 5, 7, front, right), (0, 6, 7, back, left),
    ]
    ring = [
        remote(bundle.at[route, src, part], bundle.at[route, dst, part], ring_s.at[n], ring_r.at[n], where)
        for n, (route, src, dst, part, where) in enumerate(hops)
    ]

    def assemble(route):
        row = iota((16, HD), 0)
        tile = jnp.zeros((16, HD), F32)
        for j in range(8):
            bundle[route, 0, j * HALF : (j + 1) * HALF] = stage[route, j, 0:HALF]
            bundle[route, 0, KEYS // 2 + j * HALF : KEYS // 2 + (j + 1) * HALF] = stage[route, j, HALF : 2 * HALF]
            tile = jnp.where(row == j, stage[route, j, 2 * HALF :].astype(F32), tile)
        bundle[route, 0, KEYS:] = tile.astype(BF16)

    def limits():
        lane = iota((16, HD), 1)
        own = jnp.where(lane == 0, first, jnp.where(lane == 1, second, 0.0))
        return jnp.where(lane < 4, own + pos_rx[...].astype(F32), 1e6)[0:1]

    def prepare(k, diagonal=False):
        limit = limits()
        for route in range(2):
            base = route * KEYS // 2
            keys = pl.ds(base, KEYS // 2)
            kaug[k, keys, 0:HD] = bundle[route, k, 0 : KEYS // 2]
            vt[k, 0:HD, keys] = bundle[route, k, KEYS // 2 : KEYS].T
            tile = bundle[route, k, KEYS:].astype(F32)
            for j in range(8):
                bias = jnp.broadcast_to(jnp.where(tile[j : j + 1] <= limit, 0.0, -BIG), (HALF, HD))
                if diagonal and j == 0:
                    key = iota((HALF, HD), 0) + route * HALF
                    tok = iota((HALF, HD), 1) - 4
                    late = jnp.logical_and(jnp.logical_and(tok >= 0, tok < SPAN), key > tok)
                    bias = jnp.where(late, -BIG, bias)
                kaug[k, pl.ds(base + j * HALF, HALF), HD:] = bias.astype(BF16)

    def scores(k, t):
        return jnp.dot(kaug[k], qt[:, t * TILE : (t + 1) * TILE], preferred_element_type=F32)

    def absorb(k, t):
        at = pl.ds(t * TILE, TILE)
        s = sbuf[t % 2]
        old = mx[:, at]
        new = jnp.maximum(old, jnp.max(s, axis=0, keepdims=True))
        fade = jnp.exp2((old - new) * SCALE)
        p = jnp.exp2((s - new[:1]) * SCALE).astype(BF16)
        mx[:, at] = new
        acc[:, at] = acc[:, at] * fade[:1] + jnp.dot(vt[k], p, preferred_element_type=F32)

    for copy in one:
        copy.wait_recv()
    for route in range(2):
        assemble(route)
    for n in range(5):
        ring[n].start()
    for copy in swap:
        copy.wait_recv()
    prepare(0, diagonal=True)
    sbuf[0] = scores(0, 0)

    def arrive(k):
        @pl.when(k == 1)
        def _():
            for n in range(5):
                ring[n].wait_recv()
            for n in range(5, 10):
                ring[n].start()

        @pl.when(k == 2)
        def _():
            w_got[0].wait_recv()
            w_send[1].start()
            w_send[2].start()

        @pl.when(k == 3)
        def _():
            for n in (5, 6):
                ring[n].wait_recv()
            for n in (10, 11):
                ring[n].start()

        @pl.when(k == 4)
        def _():
            for n in (7, 8):
                ring[n].wait_recv()
            ring[12].start()

        @pl.when(k == 5)
        def _():
            for n in (10, 11):
                ring[n].wait_recv()
            for n in (13, 14):
                ring[n].start()

        @pl.when(k == 6)
        def _():
            ring[9].wait_recv()
            w_got[2].wait_recv()
            w_send[3].start()

        @pl.when(k == 7)
        def _():
            for n in (12, 13, 14):
                ring[n].wait_recv()

    @pl.loop(0, 7)
    def _(k):
        for t in range(TILES):
            if t == TILES - 1:
                arrive(k + 1)
                prepare(k + 1)
                following = scores(k + 1, 0)
            else:
                following = scores(k, t + 1)
            absorb(k, t)
            sbuf[1 - t % 2] = following

    def stats(group):
        return jnp.where(iota((8, COLS), 0) < 4, mx[:, cols(group)], acc[HD : HD + 8, cols(group)])

    def merge(group, part, stat):
        there, here = stat[0:1], mx[0:1, cols(group)]
        top = jnp.maximum(there, here)
        ours, theirs = jnp.exp2((here - top) * SCALE), jnp.exp2((there - top) * SCALE)
        acc[0:HD, cols(group)] = acc[0:HD, cols(group)] * ours + part.astype(F32) * theirs
        total = acc[HD : HD + 8, cols(group)] * ours + stat[4:5] * theirs
        acc[HD : HD + 8, cols(group)] = total
        mx[:, cols(group)] = jnp.broadcast_to(top, (8, COLS))

    tail = []
    for g in range(2):
        tail.append(remote(p1_tx.at[g], p1_rx.at[g], tail_s.at[2 * g], tail_r.at[2 * g], device(dc=1)))
        tail.append(remote(s1_tx.at[g], s1_rx.at[g], tail_s.at[2 * g + 1], tail_r.at[2 * g + 1], device(dc=1)))
    tail.append(remote(p2_tx, p2_rx, tail_s.at[4], tail_r.at[4], device(dh=1)))
    tail.append(remote(s2_tx, s2_rx, tail_s.at[5], tail_r.at[5], device(dh=1)))
    tail.append(remote(c_tx, c_rx, tail_s.at[6], tail_r.at[6], device(dh=1)))

    for t in range(TILES):
        if t < TILES - 1:
            following = scores(7, t + 1)
        absorb(7, t)
        if t < TILES - 1:
            sbuf[1 - t % 2] = following
        if t == 2:
            for g in range(2):
                p1_tx[g] = acc[0:HD, cols(g)].astype(BF16)
                s1_tx[g] = stats(g)
            for n in range(4):
                tail[n].start()

    for n in (2, 3):
        tail[n].wait_recv()
    merge(2, p1_rx[1], s1_rx[1])
    p2_tx[...] = acc[0:HD, cols(2)].astype(BF16)
    s2_tx[...] = stats(2)
    tail[4].start()
    tail[5].start()
    for n in (0, 1):
        tail[n].wait_recv()
    merge(3, p1_rx[0], s1_rx[0])
    w_copy.wait()
    for n in (1, 3):
        w_got[n].wait_recv()
    for n in (4, 5):
        tail[n].wait_recv()
    merge(3, p2_rx[...], s2_rx[...])
    c_tx[...] = (acc[0:HD, cols(3)] / acc[HD : HD + 1, cols(3)]).astype(BF16)
    tail[6].start()

    def context(ref):
        flat = ref[...].T
        return jnp.concatenate([flat[i * TOK : (i + 1) * TOK] for i in range(HEADS)], axis=1)

    own = context(c_tx)

    @pl.loop(0, w_cols // TILE)
    def _(n):
        at = pl.ds(pl.multiple_of(n * TILE, TILE), TILE)
        pacc[:, at] = jnp.dot(own, w_own[:, at], preferred_element_type=F32)

    tail[6].wait_recv()
    other = context(c_rx)

    @pl.loop(0, w_cols // TILE)
    def _(n):
        at = pl.ds(pl.multiple_of(n * TILE, TILE), TILE)
        term = jnp.dot(other, w_oth[:, :, at].reshape(HEADS * HD, TILE), preferred_element_type=F32)
        o_ref[:, at] = (pacc[:, at] + term).astype(BF16)

    for copy in one + swap + ring + w_send + tail:
        copy.wait_send()


def body(queries, keys, values, span_order, w_out):
    width = w_out.shape[1] // 2
    vmem = pl.BlockSpec(memory_space=pltpu.VMEM)
    dma = pltpu.SemaphoreType.DMA
    scratch = [
        pltpu.VMEM((2 * HD, 4 * COLS), BF16),
        pltpu.VMEM((16, HD), BF16),
        pltpu.VMEM((16, HD), BF16),
        pltpu.VMEM((2, 8, 2 * HALF + 16, HD), BF16),
        pltpu.VMEM((2, 8, BUNDLE, HD), BF16),
        pltpu.VMEM((8, KEYS, 2 * HD), BF16),
        pltpu.VMEM((8, VROWS, KEYS), BF16),
        pltpu.VMEM((2, KEYS, TILE), F32),
        pltpu.VMEM((VROWS, 4 * COLS), F32),
        pltpu.VMEM((8, 4 * COLS), F32),
        pltpu.VMEM((HEADS * HD, width), BF16),
        pltpu.VMEM((HEADS, HD, width), BF16),
        pltpu.VMEM((TOK, width), F32),
        pltpu.VMEM((2, HD, COLS), BF16),
        pltpu.VMEM((2, HD, COLS), BF16),
        pltpu.VMEM((2, 8, COLS), F32),
        pltpu.VMEM((2, 8, COLS), F32),
        pltpu.VMEM((HD, COLS), BF16),
        pltpu.VMEM((HD, COLS), BF16),
        pltpu.VMEM((8, COLS), F32),
        pltpu.VMEM((8, COLS), F32),
        pltpu.VMEM((HD, COLS), BF16),
        pltpu.VMEM((HD, COLS), BF16),
        dma((2, 8)), dma((2, 8)), dma((3,)), dma((3,)), dma((2,)), dma((15,)), dma((15,)),
        dma((4,)), dma((4,)), dma, dma((7,)), dma((7,)),
    ]
    return pl.pallas_call(
        kernel,
        out_shape=jax.ShapeDtypeStruct((TOK, width), BF16),
        in_specs=[vmem, vmem, vmem, pl.BlockSpec(memory_space=pltpu.SMEM), pl.BlockSpec(memory_space=pl.ANY)],
        out_specs=vmem,
        scratch_shapes=scratch,
        compiler_params=pltpu.CompilerParams(
            collective_id=0, has_side_effects=True, vmem_limit_bytes=48 * 2**20
        ),
    )(queries, keys, values, span_order, w_out)


def solution(mesh):
    return jax.shard_map(
        body,
        mesh=mesh,
        in_specs=(P("ctx", "grp"), P("ctx", None), P("ctx", None), P("ctx"), P("grp", None)),
        out_specs=P("ctx", "grp"),
        check_vma=False,
    )
```

time: 676 us -> 76.7 us (0.11)
  waiting for transfers between devices: 301 us -> 0 us
  local copies, waits for them, and re-layouts: 157 us -> 4.12 us
  matrix products: 143 us -> 0 us
  Pallas kernels: 0 us -> 71.8 us
  other arithmetic: 34.5 us -> 0 us
  blocking collectives: 22.7 us -> 0 us
  between operations: 13.9 us -> 0.01 us
    all_gather x2 -> x0, waiting for transfers between devices: 262 us -> none  [the longest x1 219 us: body(): lax.all_gather(values, 'ctx', axis=0, tiled=True)]
    gather x2 -> x0, local copies, waits for them, and re-layouts: 154 us -> none  [global_positions(): return order_table[row_ids // span] * span + row_ids % span]
    dot_general x97 -> x0, matrix products: 143 us -> none  [the longest x48 70.2 us: absorb(): jnp.einsum('hrc,cd->hrd', weights.astype(jnp.bfloat16), value_block, pref...]
    pallas_call x0 -> x1, Pallas kernels: none -> 71.8 us  [body(): pl.pallas_call(kernel, out_shape=jax.ShapeDtypeStruct((TOK, width), BF16)...]
    reduce_scatter x1 -> x0, waiting for transfers between devices: 37.1 us -> none  [body(): lax.psum_scatter(partial_term.astype(jnp.bfloat16), 'grp', scatter_dimens...]
    reduce_sum x48 -> x0, other arithmetic: 27.2 us -> none  [absorb(): denominator = denominator * fade_factor + jnp.sum(weights, axis=-1)]
    unnamed x1 -> x0, blocking collectives: 22.7 us -> none
  transfers between devices with their start and end apart: 3 -> 0, of which waited for: 3 -> 0; matrix products, arithmetic and copies ran while one was open for 23% -> 0% of each run, Pallas kernels for 0% -> 0%
where the time goes in v1:
time: 76.7 us; the launch traced here: 75.9 us
  Pallas kernels  71.8 us (94%)
  local copies, waits for them, and re-layouts  4.12 us (5%)
    pallas_call x1, Pallas kernels, body(): pl.pallas_call(kernel, out_shape=jax.ShapeDtypeStruct((TOK, width), BF16)...  71.8 us
    unnamed x9, local copies, waits for them, and re-layouts  4.12 us

profile of v1, /device:TPU:1, one launch (start us, length us, event | category | flops | bytes accessed | tf_op | source)
XLA Modules:
  0.0 75.9 jit_solution(17922337197349708328)
XLA Ops:
  0.0 0.0 copy-start
  0.0 0.9 %copy-done = bf16[192,512]{1,0:T(8,128)(2,1)S(1)} copy-done((bf16[192,512]{1,0:T(8,128)(2,1)S(1)}, bf16[192,512]{1,0:T(8,128)(2,1)}, u32[]{:S(2)}) %copy-start) | copy-done | bytes 196632
  0.9 0.0 copy-start.1
  0.9 0.8 %copy-done.1 = bf16[192,128]{1,0:T(8,128)(2,1)S(1)} copy-done((bf16[192,128]{1,0:T(8,128)(2,1)S(1)}, bf16[192,128]{1,0:T(8,128)(2,1)}, u32[]{:S(2)}) %copy-start.1) | copy-done | bytes 49176
  1.7 0.0 copy-start.2
  1.7 0.8 %copy-done.2 = bf16[192,128]{1,0:T(8,128)(2,1)S(1)} copy-done((bf16[192,128]{1,0:T(8,128)(2,1)S(1)}, bf16[192,128]{1,0:T(8,128)(2,1)}, u32[]{:S(2)}) %copy-start.2) | copy-done | bytes 49176
  2.5 0.0 copy-start.3
  2.5 0.7 copy-done.3
  3.2 71.8 %shard_map.55 = bf16[192,2560]{1,0:T(8,128)(2,1)S(1)} custom-call(bf16[192,512]{1,0:T(8,128)(2,1)S(1)} %copy-done, bf16[192,128]{1,0:T(8,128)(2,1)S(1)} %copy-done.1, bf16[192,128]{1,0:T(8,128)(2,1)S(1)} %copy-done.2, s32[2]{0:T(128)S(1)} %copy-done.3, bf16[512,5120]{1,0:T(8,128)(2,1)} %w_ref.1), custom_call_target="tpu_custom_call" | custom-call | tf_op jit(solution)/shard_map/pallas_call | solution.py:361
  75.0 0.9 %copy.7 = bf16[192,2560]{1,0:T(8,128)(2,1)} copy(bf16[192,2560]{1,0:T(8,128)(2,1)S(1)} %shard_map.55) | data formatting | bytes 1966080
Async XLA Ops:
  0.0 0.9 %copy-start = (bf16[192,512]{1,0:T(8,128)(2,1)S(1)}, bf16[192,512]{1,0:T(8,128)(2,1)}, u32[]{:S(2)}) copy-start(bf16[192,512]{1,0:T(8,128)(2,1)} %q_ref.1) | copy-start | bytes 589828
  0.9 0.8 %copy-start.1 = (bf16[192,128]{1,0:T(8,128)(2,1)S(1)}, bf16[192,128]{1,0:T(8,128)(2,1)}, u32[]{:S(2)}) copy-start(bf16[192,128]{1,0:T(8,128)(2,1)} %k_ref.1) | copy-start | bytes 147460
  1.7 0.8 %copy-start.2 = (bf16[192,128]{1,0:T(8,128)(2,1)S(1)}, bf16[192,128]{1,0:T(8,128)(2,1)}, u32[]{:S(2)}) copy-start(bf16[192,128]{1,0:T(8,128)(2,1)} %v_ref.1) | copy-start | bytes 147460
  2.5 0.7 copy-start.3

commit v2 on v1

v2 whole, which is shorter than its diff:
```python
import functools

import jax
import jax.numpy as jnp
from jax import lax
from jax.experimental import pallas as pl
from jax.experimental.pallas import tpu as pltpu
from jax.sharding import PartitionSpec as P

HD = 128
HEADS = 4
TOK = 192
SPAN = 96
HALF = 48
COLS = HEADS * TOK
TILE = 512
TILES = 4 * COLS // TILE
PIECES = 4
PART = HD // PIECES
KEYS = 16 * HALF
BUNDLE = KEYS + 16
VROWS = 144
MESH = pl.DeviceIdType.MESH
BIG = 2.0**100
SCALE = HD**-0.5 * 1.4426950408889634
F32 = jnp.float32
BF16 = jnp.bfloat16


def iota(shape, dim):
    return lax.broadcasted_iota(jnp.int32, shape, dim)


def kernel(
    q_hbm, k_hbm, v_hbm, order_hbm, w_ref, o_ref,
    q_ref, k_ref, v_ref, order_ref,
    qt, pos_tx, pos_rx, stage, bundle, kaug, vt, sbuf, acc, mx, w_own, w_oth, pacc,
    p1_tx, p1_rx, s1_tx, s1_rx, p2_tx, p2_rx, s2_tx, s2_rx, c_tx, c_rx,
    one_s, one_r, q_s, q_r, pos_sem, ring_s, ring_r, w_s, w_r, local, tail_s, tail_r,
):
    ctx, h = lax.axis_index("ctx"), lax.axis_index("grp")
    z, ylo, x, core = ctx // 16, (ctx // 8) % 2, (ctx // 2) % 4, ctx % 2

    def device(dz=0, dy=0, dx=0, dc=0, dh=0):
        z1, x1 = (z + dz) % 8, (x + dx) % 4
        y1 = 1 - ylo if dy else ylo
        c1 = 1 - core if dc else core
        return (((z1 * 2 + y1) * 4 + x1) * 2 + c1, 1 - h if dh else h)

    def remote(src, dst, send, recv, where):
        return pltpu.make_async_remote_copy(
            src_ref=src, dst_ref=dst, send_sem=send, recv_sem=recv, device_id=where, device_id_type=MESH
        )

    plane = [(j // 4, j % 4) for j in range(1, 8)]
    mates = [(0, 0), (1, 0), (0, 1), (1, 1)]
    peers = [device(dy=dy, dx=dx) for dy, dx in plane] + [device(dz=dz) for dz in range(1, 8)]
    peers += [device(dc=dc, dh=dh) for dc, dh in mates[1:]] + [device(dy=1, dh=1)]
    barrier = pltpu.get_barrier_semaphore()
    for peer in peers:
        pl.semaphore_signal(barrier, inc=1, device_id=peer, device_id_type=MESH)

    loads = [
        pltpu.make_async_copy(src, dst, local.at[n])
        for n, (src, dst) in enumerate([(order_hbm, order_ref), (k_hbm, k_ref), (v_hbm, v_ref), (q_hbm, q_ref)])
    ]
    for copy in loads:
        copy.start()
    w_cols = w_own.shape[1]
    w_half = pl.multiple_of(h * w_cols, 128)
    w_copy = pltpu.make_async_copy(w_ref.at[:, pl.ds(w_half, w_cols)], w_own, local.at[4])
    w_copy.start()

    def cols(group):
        return pl.ds(group * COLS, COLS)

    sub = iota((HD, COLS), 0)
    col = iota((1, COLS), 1)
    token = col % TOK
    block = token // SPAN
    step_row = token % SPAN + 4
    for g in range(4):
        dc = mates[g][0]
        hit = sub == block + 2 * dc
        if dc == 0:
            hit = jnp.logical_or(hit, jnp.logical_and(sub == step_row, block == h))
        qt[HD : 2 * HD, cols(g)] = jnp.where(hit, 1.0, 0.0).astype(BF16)
    for k in range(8):
        vt[k, HD:VROWS, :] = jnp.ones((VROWS - HD, KEYS), BF16)
    acc[...] = jnp.zeros_like(acc)
    mx[...] = jnp.full_like(mx, -BIG)

    for copy in loads:
        copy.wait()
    stacked = jnp.concatenate([q_ref[:, i * HD : (i + 1) * HD] for i in range(HEADS)], axis=0)
    qt[0:HD, cols(0)] = stacked.T
    first, second = order_ref[0].astype(F32), order_ref[1].astype(F32)
    mine = jnp.where(h == 0, first, second)
    row0 = pl.multiple_of(h * SPAN, 16)
    for route in range(2):
        rows = pl.ds(pl.multiple_of(row0 + route * HALF, 16), HALF)
        stage[route, 0, 0:HALF] = k_ref[rows, :]
        stage[route, 0, HALF : 2 * HALF] = v_ref[rows, :]
        stage[route, 0, 2 * HALF :] = jnp.full((16, HD), mine, F32).astype(BF16)
    lane = iota((16, HD), 1)
    pos_tx[...] = jnp.where(lane == 2, first, jnp.where(lane == 3, second, 0.0)).astype(BF16)

    pl.semaphore_wait(barrier, len(peers))

    one = []
    for j in range(1, 8):
        dy, dx = plane[j - 1]
        for route, where in ((0, device(dy=dy, dx=dx)), (1, device(dz=j))):
            one.append(remote(stage.at[route, 0], stage.at[route, j], one_s.at[route, j], one_r.at[route, j], where))
    swap = [
        remote(qt.at[0:HD, cols(a)], qt.at[0:HD, cols(b)], q_s.at[n], q_r.at[n], where)
        for n, (a, b, where) in enumerate([(0, 1, device(dc=1)), (0, 2, device(dh=1)), (2, 3, device(dc=1))])
    ]
    swap.append(remote(pos_tx, pos_rx, pos_sem.at[0], pos_sem.at[1], device(dc=1)))
    for copy in one + swap[:2] + swap[3:]:
        copy.start()

    o_half = pl.multiple_of((1 - h) * w_cols, 128)
    quarter, far = 2 * ylo + core, 2 * (1 - ylo) + core
    cross, pass_core, pass_y, relay, got_core, got_y, got_relay = [], [], [], [], [], [], []
    for i in range(PIECES):
        rows = pl.ds(pl.multiple_of(far * HD + i * PART, PART), PART)
        part = pl.ds(i * PART, PART)
        w_from = w_ref.at[rows, pl.ds(o_half, w_cols)]
        mine_w, far_w = w_oth.at[quarter, part], w_oth.at[far, part]
        near_w, last_w = w_oth.at[2 * ylo + 1 - core, part], w_oth.at[2 * (1 - ylo) + 1 - core, part]
        cross.append(remote(w_from, far_w, w_s.at[0, i], w_r.at[0, i], device(dy=1, dh=1)))
        pass_core.append(remote(mine_w, mine_w, w_s.at[1, i], w_r.at[1, i], device(dc=1)))
        pass_y.append(remote(mine_w, mine_w, w_s.at[2, i], w_r.at[2, i], device(dy=1)))
        relay.append(remote(far_w, far_w, w_s.at[3, i], w_r.at[3, i], device(dc=1)))
        got_core.append(remote(mine_w, near_w, w_s.at[1, i], w_r.at[1, i], device(dc=1)))
        got_y.append(remote(mine_w, far_w, w_s.at[2, i], w_r.at[2, i], device(dy=1)))
        got_relay.append(remote(far_w, last_w, w_s.at[3, i], w_r.at[3, i], device(dc=1)))
    got_cross = [
        remote(w_from, w_oth.at[quarter, pl.ds(i * PART, PART)], w_s.at[0, i], w_r.at[0, i], device(dy=1, dh=1))
        for i in range(PIECES)
    ]
    cross[0].start()
    cross[1].start()

    right, left, up, down, over = device(dz=1), device(dz=7), device(dx=1), device(dx=3), device(dy=1)
    whole, front, back = pl.ds(0, BUNDLE), pl.ds(0, KEYS // 2), pl.ds(KEYS // 2, BUNDLE - KEYS // 2)
    hops = [
        (0, 0, 1, whole, right), (0, 0, 2, whole, left), (1, 0, 1, whole, up), (1, 0, 2, whole, down), (1, 0, 3, whole, over),
        (0, 1, 3, whole, right), (0, 2, 4, whole, left), (1, 3, 4, whole, up), (1, 3, 5, whole, down), (1, 1, 6, whole, up),
        (0, 3, 5, whole, right), (0, 4, 6, whole, left), (1, 5, 7, whole, down),
        (0, 5, 7, front, right), (0, 6, 7, back, left),
    ]
    ring = [
        remote(bundle.at[route, src, part], bundle.at[route, dst, part], ring_s.at[n], ring_r.at[n], where)
        for n, (route, src, dst, part, where) in enumerate(hops)
    ]

    def assemble(route):
        row = iota((16, HD), 0)
        tile = jnp.zeros((16, HD), F32)
        for j in range(8):
            bundle[route, 0, j * HALF : (j + 1) * HALF] = stage[route, j, 0:HALF]
            bundle[route, 0, KEYS // 2 + j * HALF : KEYS // 2 + (j + 1) * HALF] = stage[route, j, HALF : 2 * HALF]
            tile = jnp.where(row == j, stage[route, j, 2 * HALF :].astype(F32), tile)
        bundle[route, 0, KEYS:] = tile.astype(BF16)

    def limits():
        lane = iota((16, HD), 1)
        own = jnp.where(lane == 0, first, jnp.where(lane == 1, second, 0.0))
        return jnp.where(lane < 4, own + pos_rx[...].astype(F32), 1e6)[0:1]

    def prepare(k, diagonal=False):
        limit = limits()
        for route in range(2):
            base = route * KEYS // 2
            keys = pl.ds(base, KEYS // 2)
            kaug[k, keys, 0:HD] = bundle[route, k, 0 : KEYS // 2]
            vt[k, 0:HD, keys] = bundle[route, k, KEYS // 2 : KEYS].T
            tile = bundle[route, k, KEYS:].astype(F32)
            for j in range(8):
                bias = jnp.broadcast_to(jnp.where(tile[j : j + 1] <= limit, 0.0, -BIG), (HALF, HD))
                if diagonal and j == 0:
                    key = iota((HALF, HD), 0) + route * HALF
                    tok = iota((HALF, HD), 1) - 4
                    late = jnp.logical_and(jnp.logical_and(tok >= 0, tok < SPAN), key > tok)
                    bias = jnp.where(late, -BIG, bias)
                kaug[k, pl.ds(base + j * HALF, HALF), HD:] = bias.astype(BF16)

    def scores(k, t):
        at = pl.ds(t * TILE, TILE) if isinstance(t, int) else pl.ds(pl.multiple_of(t * TILE, TILE), TILE)
        return jnp.dot(kaug[k], qt[:, at], preferred_element_type=F32)

    def absorb(k, t, slot):
        at = pl.ds(t * TILE, TILE)
        s = sbuf[slot]
        old = mx[:, at]
        new = jnp.maximum(old, jnp.max(s, axis=0, keepdims=True))
        fade = jnp.exp2((old - new) * SCALE)
        p = jnp.exp2((s - new[:1]) * SCALE).astype(BF16)
        mx[:, at] = new
        acc[:, at] = acc[:, at] * fade[:1] + jnp.dot(vt[k], p, preferred_element_type=F32)

    for route, first_hops in ((0, (0, 1)), (1, (2, 3, 4))):
        for copy in one[route::2]:
            copy.wait_recv()
        assemble(route)
        for n in first_hops:
            ring[n].start()
    swap[3].wait_recv()
    prepare(0, diagonal=True)
    sbuf[0] = scores(0, 0)

    def arrive(k):
        def receive(*hops):
            for n in hops:
                ring[n].wait_recv()

        def forward(*hops):
            for n in hops:
                ring[n].start()

        def w_on(i):
            got_cross[i].wait_recv()
            pass_y[i].start()
            pass_core[i].start()

        def w_over(i):
            got_y[i].wait_recv()
            relay[i].start()

        @pl.when(k == 1)
        def _():
            receive(0, 1, 2, 3, 4)
            forward(5, 6, 7, 8, 9)

        @pl.when(k == 2)
        def _():
            w_on(0)
            cross[2].start()

        @pl.when(k == 3)
        def _():
            receive(5, 6)
            forward(10, 11)
            w_on(1)
            cross[3].start()

        @pl.when(k == 4)
        def _():
            receive(7, 8)
            forward(12)
            w_on(2)
            w_over(0)

        @pl.when(k == 5)
        def _():
            receive(10, 11)
            forward(13, 14)
            w_on(3)
            w_over(1)

        @pl.when(k == 6)
        def _():
            receive(9, 12, 13, 14)
            w_over(2)

    def step(now, following, slot):
        ahead = scores(*following)
        absorb(*now, slot)
        sbuf[1 - slot] = ahead

    for t in range(TILES - 1):
        if t == 0:
            swap[0].wait_recv()
        if t == 2:
            swap[1].wait_recv()
            swap[2].start()
        if t == 3:
            swap[2].wait_recv()
        step((0, t), (0, t + 1), t % 2)
    arrive(1)
    prepare(1)
    step((0, TILES - 1), (1, 0), 1)

    @pl.loop(1, 6)
    def _(k):
        for t in range(TILES - 1):
            step((k, t), (k, t + 1), t % 2)
        arrive(k + 1)
        prepare(k + 1)
        step((k, TILES - 1), (k + 1, jnp.where(k == 5, TILES - 1, 0)), 1)

    prepare(7)

    def stats(group):
        return jnp.where(iota((8, COLS), 0) < 4, mx[:, cols(group)], acc[HD : HD + 8, cols(group)])

    def merge(group, part, stat):
        there, here = stat[0:1], mx[0:1, cols(group)]
        top = jnp.maximum(there, here)
        ours, theirs = jnp.exp2((here - top) * SCALE), jnp.exp2((there - top) * SCALE)
        acc[0:HD, cols(group)] = acc[0:HD, cols(group)] * ours + part.astype(F32) * theirs
        total = acc[HD : HD + 8, cols(group)] * ours + stat[4:5] * theirs
        acc[HD : HD + 8, cols(group)] = total
        mx[:, cols(group)] = jnp.broadcast_to(top, (8, COLS))

    tail = []
    for n, (src, dst, where) in enumerate([
        (p1_tx.at[0], p1_rx.at[0], device(dc=1)), (s1_tx.at[0], s1_rx.at[0], device(dc=1)),
        (p1_tx.at[1], p1_rx.at[1], device(dc=1)), (s1_tx.at[1], s1_rx.at[1], device(dc=1)),
        (p2_tx, p2_rx, device(dh=1)), (s2_tx, s2_rx, device(dh=1)), (c_tx, c_rx, device(dh=1)),
    ]):
        tail.append(remote(src, dst, tail_s.at[n], tail_r.at[n], where))

    def hand_over(n, group):
        p1_tx[n] = acc[0:HD, cols(group)].astype(BF16)
        s1_tx[n] = stats(group)
        tail[2 * n].start()
        tail[2 * n + 1].start()

    order = [(k, t) for t in reversed(range(TILES)) for k in (6, 7)]
    for n, now in enumerate(order):
        if n + 1 < len(order):
            step(now, order[n + 1], n % 2)
        else:
            absorb(*now, n % 2)
        if now == (7, 4):
            hand_over(0, 3)
        if now == (7, 2):
            tail[0].wait_recv()
            tail[1].wait_recv()
            merge(2, p1_rx[0], s1_rx[0])
            p2_tx[...] = acc[0:HD, cols(2)].astype(BF16)
            s2_tx[...] = stats(2)
            tail[4].start()
            tail[5].start()
            got_y[3].wait_recv()
            relay[3].start()
        if now == (7, 1):
            hand_over(1, 1)

    for n in (2, 3):
        tail[n].wait_recv()
    merge(0, p1_rx[1], s1_rx[1])
    for n in (4, 5):
        tail[n].wait_recv()
    merge(0, p2_rx[...], s2_rx[...])
    c_tx[...] = (acc[0:HD, cols(0)] / acc[HD : HD + 1, cols(0)]).astype(BF16)
    tail[6].start()
    w_copy.wait()
    for copy in got_core + got_relay:
        copy.wait_recv()

    def context(ref):
        flat = ref[...].T
        return jnp.concatenate([flat[i * TOK : (i + 1) * TOK] for i in range(HEADS)], axis=1)

    own = context(c_tx)

    @pl.loop(0, w_cols // TILE)
    def _(n):
        at = pl.ds(pl.multiple_of(n * TILE, TILE), TILE)
        pacc[:, at] = jnp.dot(own, w_own[:, at], preferred_element_type=F32)

    tail[6].wait_recv()
    other = context(c_rx)

    @pl.loop(0, w_cols // TILE)
    def _(n):
        at = pl.ds(pl.multiple_of(n * TILE, TILE), TILE)
        term = jnp.dot(other, w_oth[:, :, at].reshape(HEADS * HD, TILE), preferred_element_type=F32)
        o_ref[:, at] = (pacc[:, at] + term).astype(BF16)

    for copy in one + swap + ring + cross + pass_core + pass_y + relay + tail:
        copy.wait_send()


def body(queries, keys, values, span_order, w_out):
    width = w_out.shape[1] // 2
    vmem = pl.BlockSpec(memory_space=pltpu.VMEM)
    dma = pltpu.SemaphoreType.DMA
    scratch = [
        pltpu.VMEM((TOK, HEADS * HD), BF16),
        pltpu.VMEM((TOK, HD), BF16),
        pltpu.VMEM((TOK, HD), BF16),
        pltpu.SMEM((2,), jnp.int32),
        pltpu.VMEM((2 * HD, 4 * COLS), BF16),
        pltpu.VMEM((16, HD), BF16),
        pltpu.VMEM((16, HD), BF16),
        pltpu.VMEM((2, 8, 2 * HALF + 16, HD), BF16),
        pltpu.VMEM((2, 8, BUNDLE, HD), BF16),
        pltpu.VMEM((8, KEYS, 2 * HD), BF16),
        pltpu.VMEM((8, VROWS, KEYS), BF16),
        pltpu.VMEM((2, KEYS, TILE), F32),
        pltpu.VMEM((VROWS, 4 * COLS), F32),
        pltpu.VMEM((8, 4 * COLS), F32),
        pltpu.VMEM((HEADS * HD, width), BF16),
        pltpu.VMEM((HEADS, HD, width), BF16),
        pltpu.VMEM((TOK, width), F32),
        pltpu.VMEM((2, HD, COLS), BF16),
        pltpu.VMEM((2, HD, COLS), BF16),
        pltpu.VMEM((2, 8, COLS), F32),
        pltpu.VMEM((2, 8, COLS), F32),
        pltpu.VMEM((HD, COLS), BF16),
        pltpu.VMEM((HD, COLS), BF16),
        pltpu.VMEM((8, COLS), F32),
        pltpu.VMEM((8, COLS), F32),
        pltpu.VMEM((HD, COLS), BF16),
        pltpu.VMEM((HD, COLS), BF16),
        dma((2, 8)), dma((2, 8)), dma((3,)), dma((3,)), dma((2,)), dma((15,)), dma((15,)),
        dma((4, PIECES)), dma((4, PIECES)), dma((5,)), dma((7,)), dma((7,)),
    ]
    return pl.pallas_call(
        kernel,
        out_shape=jax.ShapeDtypeStruct((TOK, width), BF16),
        in_specs=[pl.BlockSpec(memory_space=pl.ANY)] * 5,
        out_specs=vmem,
        scratch_shapes=scratch,
        compiler_params=pltpu.CompilerParams(
            collective_id=0, has_side_effects=True, vmem_limit_bytes=56 * 2**20
        ),
    )(queries, keys, values, span_order, w_out)


def solution(mesh):
    return jax.shard_map(
        body,
        mesh=mesh,
        in_specs=(P("ctx", "grp"), P("ctx", None), P("ctx", None), P("ctx"), P("grp", None)),
        out_specs=P("ctx", "grp"),
        check_vma=False,
    )
```

time: 76.7 us -> 62.1 us (0.81)
  Pallas kernels: 71.8 us -> 59.7 us
  local copies, waits for them, and re-layouts: 4.12 us -> 2.21 us
    pallas_call x1, Pallas kernels: 71.8 us -> 59.7 us  [body(): pl.pallas_call(kernel, out_shape=jax.ShapeDtypeStruct((TOK, width), BF16)...]
    unnamed x9 -> x1, local copies, waits for them, and re-layouts: 4.12 us -> 2.21 us
where the time goes in v2:
time: 62.1 us; the launch traced here: 61.9 us
  Pallas kernels  59.7 us (96%)
  local copies, waits for them, and re-layouts  2.21 us (4%)
    pallas_call x1, Pallas kernels, body(): pl.pallas_call(kernel, out_shape=jax.ShapeDtypeStruct((TOK, width), BF16)...  59.7 us
    unnamed x1, local copies, waits for them, and re-layouts  2.21 us

profile of v2, /device:TPU:1, one launch (start us, length us, event | category | flops | bytes accessed | tf_op | source)
XLA Modules:
  0.0 61.9 jit_solution(12429143173704673551)
XLA Ops:
  0.0 59.7 %shard_map.55 = bf16[192,2560]{1,0:T(8,128)(2,1)} custom-call(bf16[192,512]{1,0:T(8,128)(2,1)} %q_hbm.1, bf16[192,128]{1,0:T(8,128)(2,1)} %k_hbm.1, bf16[192,128]{1,0:T(8,128)(2,1)} %v_hbm.1, s32[2]{0:T(128)} %order_hbm.1, bf16[512,5120]{1,0:T(8,128)(2,1)} %w_ref.1), custom_call_target="tpu_custom_call" | custom-call | tf_op jit(solution)/shard_map/pallas_call | solution.py:414
  59.7 2.2 %copy.7 = bf16[192,2560]{1,0:T(8,128)(2,1)} copy(bf16[192,2560]{1,0:T(8,128)(2,1)} %shard_map.55) | data formatting | bytes 1966080

commit v3 on v0

v3 whole, which is shorter than its diff:
```python
import functools

import jax
import jax.numpy as jnp
from jax import lax
from jax.experimental import pallas as pl
from jax.experimental.pallas import tpu as pltpu
from jax.sharding import PartitionSpec as P

HD = 128
HEADS = 4
TOK = 192
SPAN = 96
SPLIT = (64, 32)
BLOCKS = (4, 8)
COLS = HEADS * TOK
UNIT = 256
TILE = 512
GROUPS = 8
TILES = GROUPS * COLS // TILE
KEYS = 3 * UNIT
CHUNKS = 4
BUNDLE = 2 * UNIT + 16
VROWS = 144
MESH = pl.DeviceIdType.MESH
BIG = 2.0**100
SCALE = HD**-0.5 * 1.4426950408889634
F32 = jnp.float32
BF16 = jnp.bfloat16


def iota(shape, dim):
    return lax.broadcasted_iota(jnp.int32, shape, dim)


def kernel(
    q_hbm, k_hbm, v_hbm, order_hbm, w_ref, o_ref,
    q_ref, k_ref, v_ref, order_ref,
    qt, pos_tx, pos_rx, stage_a, stage_b, bundle_a, bundle_b, kaug, vt, sbuf, acc, mx, w_own, w_oth, pacc,
    p1_tx, p1_rx, s1_tx, s1_rx, p2_tx, p2_rx, s2_tx, s2_rx, c_tx, c_rx,
    one_s, one_r, q_s, q_r, pos_s, pos_r, ring_s, ring_r, w_s, w_r, local, d_s, d_r, e_s, e_r, tail_sem,
):
    ctx, h = lax.axis_index("ctx"), lax.axis_index("grp")
    z, ylo, x, core = ctx // 16, (ctx // 8) % 2, (ctx // 2) % 4, ctx % 2
    y = 2 * h + ylo

    def device(dz=0, dy=0, dx=0, dc=0):
        z1, x1, y1 = (z + dz) % 8, (x + dx) % 4, (y + dy) % 4
        c1 = 1 - core if dc else core
        return (((z1 * 2 + y1 % 2) * 4 + x1) * 2 + c1, y1 // 2)

    beside = 1 - 2 * ylo + 4
    across = 3 - 2 * y + 4

    def remote(src, dst, send, recv, where):
        return pltpu.make_async_remote_copy(
            src_ref=src, dst_ref=dst, send_sem=send, recv_sem=recv, device_id=where, device_id_type=MESH
        )

    shift, lands = (0, 1, 3, 2), (0, 2, 1, 3)
    peers = [device(dx=d) for d in (1, 2, 3)] + [device(dz=d) for d in range(1, 8)]
    peers += [device(dy=d) for d in (1, 2, 3)] + [device(dc=1), device(dy=beside, dc=1)]
    barrier = pltpu.get_barrier_semaphore()
    for peer in peers:
        pl.semaphore_signal(barrier, inc=1, device_id=peer, device_id_type=MESH)

    loads = [
        pltpu.make_async_copy(src, dst, local.at[n])
        for n, (src, dst) in enumerate([(order_hbm, order_ref), (k_hbm, k_ref), (v_hbm, v_ref), (q_hbm, q_ref)])
    ]
    for copy in loads:
        copy.start()
    w_cols = w_own.shape[1]
    w_half = pl.multiple_of(h * w_cols, 128)
    w_copy = pltpu.make_async_copy(w_ref.at[:, pl.ds(w_half, w_cols)], w_own, local.at[4])
    w_copy.start()

    def cols(group):
        if isinstance(group, int):
            return pl.ds(group * COLS, COLS)
        return pl.ds(pl.multiple_of(group * COLS, COLS), COLS)

    sub = iota((HD, COLS), 0)
    col = iota((1, COLS), 1)
    token = col % TOK
    block = token // SPAN
    step_row = token % SPAN + 8

    @pl.loop(0, GROUPS)
    def _(g):
        far_y = jnp.logical_or(g // 2 == 1, g // 2 == 2)
        hit = sub == block + 2 * (g % 2) + jnp.where(far_y, 4, 0)
        same = jnp.logical_or(g == 0, g == GROUPS - 2)
        hit = jnp.logical_or(hit, jnp.logical_and(sub == step_row, block == jnp.where(same, h, -1)))
        qt[HD : 2 * HD, cols(g)] = jnp.where(hit, 1.0, 0.0).astype(BF16)

    for k in range(CHUNKS):
        vt[k, HD:VROWS, :] = jnp.ones((VROWS - HD, KEYS), BF16)

    @pl.loop(0, TILES)
    def _(t):
        at = pl.ds(pl.multiple_of(t * TILE, TILE), TILE)
        acc[:, at] = jnp.zeros((VROWS, TILE), F32)
        mx[:, at] = jnp.full((8, TILE), -BIG, F32)

    for copy in loads:
        copy.wait()
    stacked = jnp.concatenate([q_ref[:, i * HD : (i + 1) * HD] for i in range(HEADS)], axis=0)
    qt[0:HD, cols(0)] = stacked.T
    first, second = order_ref[0].astype(F32), order_ref[1].astype(F32)
    mine = jnp.where(h == 0, first, second)
    row0 = pl.multiple_of(h * SPAN, 16)
    for stage, size, start in ((stage_a, SPLIT[0], 0), (stage_b, SPLIT[1], SPLIT[0])):
        rows = pl.ds(pl.multiple_of(row0 + start, 16), size)
        stage[0, 0:size] = k_ref[rows, :]
        stage[0, size : 2 * size] = v_ref[rows, :]
        stage[0, 2 * size :] = jnp.full((16, HD), mine, F32).astype(BF16)
    pos_tx[...] = jnp.where(iota((16, HD), 1) % 2 == 0, first, second).astype(BF16)

    pl.semaphore_wait(barrier, len(peers))

    one_a = [remote(stage_a.at[0], stage_a.at[d], one_s.at[0, d], one_r.at[0, d], device(dx=d)) for d in (1, 2, 3)]
    one_b = [remote(stage_b.at[0], stage_b.at[d], one_s.at[1, d], one_r.at[1, d], device(dz=d)) for d in range(1, 8)]
    places = [
        remote(pos_tx, pos_rx.at[n], pos_s.at[n], pos_r.at[n], where)
        for n, where in enumerate([device(dc=1), device(dy=beside), device(dy=beside, dc=1)])
    ]
    q_core = remote(qt.at[0:HD, cols(0)], qt.at[0:HD, cols(1)], q_s.at[0], q_r.at[0], device(dc=1))
    q_far, q_got, q_on = [None], [None], [None]
    for j in (1, 2, 3):
        to = lands[j]
        q_far.append(remote(qt.at[0:HD, cols(0)], qt.at[0:HD, cols(2 * to)], q_s.at[j], q_r.at[to], device(dy=shift[j])))
        q_got.append(remote(qt.at[0:HD, cols(0)], qt.at[0:HD, cols(2 * j)], q_s.at[j], q_r.at[j], device(dy=shift[j])))
        q_on.append(
            remote(qt.at[0:HD, cols(2 * j)], qt.at[0:HD, cols(2 * j + 1)], q_s.at[3 + j], q_r.at[3 + j], device(dc=1))
        )
    for copy in one_a + one_b + places + [q_core] + q_far[1:3]:
        copy.start()

    o_half = pl.multiple_of((1 - h) * w_cols, 128)
    w_rows = HD // 2

    def w_part(d, c):
        return w_oth.at[(x + d) % 4, pl.ds(pl.multiple_of(c * w_rows, w_rows), w_rows)]

    w_from = w_ref.at[pl.ds(pl.multiple_of(x * HD + core * w_rows, w_rows), w_rows), pl.ds(o_half, w_cols)]
    w_cross = remote(w_from, w_part(0, core), w_s.at[0], w_r.at[0], device(dy=across))
    w_x = [remote(w_part(0, core), w_part(0, core), w_s.at[d], w_r.at[d], device(dx=d)) for d in (1, 2, 3)]
    w_x_got = [remote(w_part(0, core), w_part(4 - d, core), w_s.at[d], w_r.at[d], device(dx=d)) for d in (1, 2, 3)]
    w_on = [remote(w_part(d, core), w_part(d, core), w_s.at[4 + d], w_r.at[4 + d], device(dc=1)) for d in range(4)]
    w_on_got = [
        remote(w_part(d, core), w_part(d, 1 - core), w_s.at[4 + d], w_r.at[4 + d], device(dc=1)) for d in range(4)
    ]

    right, left, up, down = device(dz=1), device(dz=7), device(dx=1), device(dx=3)
    whole, front, back = pl.ds(0, BUNDLE), pl.ds(0, UNIT), pl.ds(UNIT, BUNDLE - UNIT)
    hops = [
        (bundle_a, 0, 1, whole, right), (bundle_a, 0, 2, whole, left), (bundle_b, 0, 1, whole, up), (bundle_b, 0, 2, whole, down),
        (bundle_a, 1, 3, whole, right), (bundle_a, 2, 4, whole, left), (bundle_b, 1, 3, front, up), (bundle_b, 2, 3, back, down),
        (bundle_a, 3, 5, whole, right), (bundle_a, 4, 6, whole, left),
        (bundle_a, 5, 7, front, right), (bundle_a, 6, 7, back, left),
    ]
    ring = [
        remote(bundle.at[src, part], bundle.at[dst, part], ring_s.at[n], ring_r.at[n], where)
        for n, (bundle, src, dst, part, where) in enumerate(hops)
    ]

    def assemble(bundle, stage, blocks, size):
        row = iota((16, HD), 0)
        tile = jnp.zeros((16, HD), F32)
        for j in range(blocks):
            bundle[0, j * size : (j + 1) * size] = stage[j, 0:size]
            bundle[0, UNIT + j * size : UNIT + (j + 1) * size] = stage[j, size : 2 * size]
            tile = jnp.where(row == j, stage[j, 2 * size :].astype(F32), tile)
        bundle[0, 2 * UNIT :] = tile.astype(BF16)

    def prepare(k):
        pair = iota((16, HD), 1) // 2
        limit = jnp.full((16, HD), 1e6, F32)
        for n, tile in enumerate([pos_tx[...], pos_rx[0], pos_rx[1], pos_rx[2]]):
            limit = jnp.where(pair == n, tile.astype(F32), limit)
        limit = limit[0:1]
        for n, (bundle, at, route) in enumerate([(bundle_a, 2 * k, 0), (bundle_a, 2 * k + 1, 0), (bundle_b, k, 1)]):
            base, size = n * UNIT, SPLIT[route]
            kaug[k, base : base + UNIT, 0:HD] = bundle[at, 0:UNIT]
            vt[k, 0:HD, base : base + UNIT] = bundle[at, UNIT : 2 * UNIT].T
            tile = bundle[at, 2 * UNIT :].astype(F32)
            for j in range(BLOCKS[route]):
                bias = jnp.broadcast_to(jnp.where(tile[j : j + 1] <= limit, 0.0, -BIG), (size, HD))
                if isinstance(k, int) and k == 0 and j == 0 and n != 1:
                    key = iota((size, HD), 0) + (SPLIT[0] if route else 0)
                    tok = iota((size, HD), 1) - 8
                    late = jnp.logical_and(jnp.logical_and(tok >= 0, tok < SPAN), key > tok)
                    bias = jnp.where(late, -BIG, bias)
                kaug[k, base + j * size : base + (j + 1) * size, HD:] = bias.astype(BF16)

    def tile_at(t):
        return pl.ds(t * TILE, TILE) if isinstance(t, int) else pl.ds(pl.multiple_of(t * TILE, TILE), TILE)

    def scores(k, t, slot):
        s = jnp.dot(kaug[k], qt[:, tile_at(t)], preferred_element_type=F32)
        sbuf[slot] = s
        return jnp.max(s, axis=0, keepdims=True)

    def step(now, following, slot, top):
        k, t = now
        at = tile_at(t)
        old = mx[:, at]
        new = jnp.maximum(old, top)
        fade = jnp.exp2((old - new) * SCALE)
        mx[:, at] = new
        if following is not None:
            top = scores(*following, 1 - slot)
        p = jnp.exp2((sbuf[slot] - new[:1]) * SCALE).astype(BF16)
        acc[:, at] = acc[:, at] * fade[:1] + jnp.dot(vt[k], p, preferred_element_type=F32)
        return top

    def receive(*copies):
        for copy in copies:
            copy.wait_recv()

    def start(*copies):
        for copy in copies:
            copy.start()

    def stats(group):
        return jnp.where(iota((8, COLS), 0) < 4, mx[:, cols(group)], acc[HD : HD + 8, cols(group)])

    def merge(group, part, stat):
        there, here = stat[0:1], mx[0:1, cols(group)]
        top = jnp.maximum(there, here)
        ours, theirs = jnp.exp2((here - top) * SCALE), jnp.exp2((there - top) * SCALE)
        acc[0:HD, cols(group)] = acc[0:HD, cols(group)] * ours + part.astype(F32) * theirs
        total = acc[HD : HD + 8, cols(group)] * ours + stat[4:5] * theirs
        acc[HD : HD + 8, cols(group)] = total
        mx[:, cols(group)] = jnp.broadcast_to(top, (8, COLS))

    def part_copies(j):
        return (
            remote(p1_tx.at[j], p1_rx.at[j], d_s.at[0, j], d_r.at[0, j], device(dc=1)),
            remote(s1_tx.at[j], s1_rx.at[j], d_s.at[1, j], d_r.at[1, j], device(dc=1)),
        )

    def sum_copies(j, to, where):
        return (
            remote(p2_tx.at[j], p2_rx.at[to], e_s.at[0, j], e_r.at[0, to], where),
            remote(s2_tx.at[j], s2_rx.at[to], e_s.at[1, j], e_r.at[1, to], where),
        )

    c_copy = remote(c_tx, c_rx, tail_sem.at[0], tail_sem.at[1], device(dy=2))

    def hand_over(j):
        p1_tx[j] = acc[0:HD, cols(2 * j + 1)].astype(BF16)
        s1_tx[j] = stats(2 * j + 1)
        start(*part_copies(j))

    def send_sum(j):
        receive(*part_copies(j))
        merge(2 * j, p1_rx[j], s1_rx[j])
        p2_tx[j] = acc[0:HD, cols(2 * j)].astype(BF16)
        s2_tx[j] = stats(2 * j)
        turn = j + (j // 2) * (5 - 2 * j)
        to = 3 * (j // 3) + (1 - j // 3) * (3 - j)
        start(*sum_copies(j, to, device(dy=turn)))

    receive(*one_a)
    start(q_far[3])
    assemble(bundle_a, stage_a, BLOCKS[0], SPLIT[0])
    start(ring[0], ring[1])
    receive(*one_b)
    assemble(bundle_b, stage_b, BLOCKS[1], SPLIT[1])
    start(ring[2], ring[3])
    receive(*places)
    receive(ring[0], ring[1])
    start(ring[4], ring[5])
    receive(q_got[1])
    start(q_on[1])
    prepare(0)
    top = scores(0, 0, 0)

    for t in range(TILES):
        if t == 0:
            receive(q_core, q_got[2])
            start(q_on[2])
        if t == 2:
            receive(q_on[1])
        if t == 3:
            start(w_cross)
        if t == 5:
            receive(q_on[2], q_got[3])
            start(q_on[3])
        if t == 9:
            receive(q_on[3], ring[2], ring[3], ring[4], ring[5])
            start(ring[6], ring[7], ring[8], ring[9])
        if t == TILES - 1:
            prepare(1)
        top = step((0, t), (0, t + 1) if t < TILES - 1 else (1, 0), t % 2, top)

    def second(i, top):
        base = i * 6
        for t in range(6):
            if t == 1:
                @pl.when(i == 1)
                def _():
                    receive(ring[8], ring[9])
                    start(ring[10], ring[11])
            if t == 5:
                @pl.when(i == 1)
                def _():
                    prepare(2)
                    receive(w_cross)
                    start(*w_x, w_on[0])
                following = (jnp.where(i == 1, 2, 1), jnp.where(i == 1, TILES - 1, 6))
            else:
                following = (1, base + t + 1)
            top = step((1, base + t), following, t % 2, top)
        return top

    top = lax.fori_loop(0, 2, second, top)
    receive(ring[6], ring[7], ring[10], ring[11])
    prepare(3)

    def far(i, top):
        j = 3 - i
        base = 3 * j
        for n in range(6):
            k, t = 2 + n % 2, base + 2 - n // 2
            if n == 2:
                pl.when(i > 0)(lambda: send_sum(j + 1))
            if n == 4:
                hand_over(j)
            following = (2 + (n + 1) % 2, base + 2 - (n + 1) // 2) if n < 5 else (2, base - 1)
            top = step((k, t), following, n % 2, top)
        return top

    top = lax.fori_loop(0, 3, far, top)
    for n in range(6):
        k, t = 2 + n % 2, 2 - n // 2
        if n == 2:
            send_sum(1)
        if n == 4:
            hand_over(0)
        top = step((k, t), (2 + (n + 1) % 2, 2 - (n + 1) // 2) if n < 5 else None, n % 2, top)

    receive(*part_copies(0))
    merge(0, p1_rx[0], s1_rx[0])
    for j in (3, 2, 1):
        receive(*sum_copies(j, j, device(dy=1)))
        merge(0, p2_rx[j], s2_rx[j])
    c_tx[...] = (acc[0:HD, cols(0)] / acc[HD : HD + 1, cols(0)]).astype(BF16)
    c_copy.start()
    receive(*w_x_got)
    start(*w_on[1:])
    w_copy.wait()

    def context(ref):
        flat = ref[...].T
        return jnp.concatenate([flat[i * TOK : (i + 1) * TOK] for i in range(HEADS)], axis=1)

    own = context(c_tx)

    @pl.loop(0, w_cols // TILE)
    def _(n):
        at = pl.ds(pl.multiple_of(n * TILE, TILE), TILE)
        pacc[:, at] = jnp.dot(own, w_own[:, at], preferred_element_type=F32)

    receive(c_copy, *w_on_got)
    other = context(c_rx)

    @pl.loop(0, w_cols // TILE)
    def _(n):
        at = pl.ds(pl.multiple_of(n * TILE, TILE), TILE)
        term = jnp.dot(other, w_oth[:, :, at].reshape(HEADS * HD, TILE), preferred_element_type=F32)
        o_ref[:, at] = (pacc[:, at] + term).astype(BF16)

    sent = one_a + one_b + places + [q_core] + q_far[1:] + q_on[1:] + ring + [w_cross] + w_x + w_on + [c_copy]
    for j in range(4):
        sent += part_copies(j)
    for j in (1, 2, 3):
        sent += sum_copies(j, lands[j], device(dy=shift[j]))
    for copy in sent:
        copy.wait_send()


def body(queries, keys, values, span_order, w_out):
    width = w_out.shape[1] // 2
    vmem = pl.BlockSpec(memory_space=pltpu.VMEM)
    dma = pltpu.SemaphoreType.DMA
    scratch = [
        pltpu.VMEM((TOK, HEADS * HD), BF16),
        pltpu.VMEM((TOK, HD), BF16),
        pltpu.VMEM((TOK, HD), BF16),
        pltpu.SMEM((2,), jnp.int32),
        pltpu.VMEM((2 * HD, GROUPS * COLS), BF16),
        pltpu.VMEM((16, HD), BF16),
        pltpu.VMEM((3, 16, HD), BF16),
        pltpu.VMEM((4, 2 * SPLIT[0] + 16, HD), BF16),
        pltpu.VMEM((8, 2 * SPLIT[1] + 16, HD), BF16),
        pltpu.VMEM((8, BUNDLE, HD), BF16),
        pltpu.VMEM((4, BUNDLE, HD), BF16),
        pltpu.VMEM((CHUNKS, KEYS, 2 * HD), BF16),
        pltpu.VMEM((CHUNKS, VROWS, KEYS), BF16),
        pltpu.VMEM((2, KEYS, TILE), F32),
        pltpu.VMEM((VROWS, GROUPS * COLS), F32),
        pltpu.VMEM((8, GROUPS * COLS), F32),
        pltpu.VMEM((HEADS * HD, width), BF16),
        pltpu.VMEM((HEADS, HD, width), BF16),
        pltpu.VMEM((TOK, width), F32),
        pltpu.VMEM((4, HD, COLS), BF16),
        pltpu.VMEM((4, HD, COLS), BF16),
        pltpu.VMEM((4, 8, COLS), F32),
        pltpu.VMEM((4, 8, COLS), F32),
        pltpu.VMEM((4, HD, COLS), BF16),
        pltpu.VMEM((4, HD, COLS), BF16),
        pltpu.VMEM((4, 8, COLS), F32),
        pltpu.VMEM((4, 8, COLS), F32),
        pltpu.VMEM((HD, COLS), BF16),
        pltpu.VMEM((HD, COLS), BF16),
        dma((2, 8)), dma((2, 8)), dma((7,)), dma((7,)), dma((3,)), dma((3,)), dma((12,)), dma((12,)), dma((8,)), dma((8,)),
        dma((5,)), dma((2, 4)), dma((2, 4)), dma((2, 4)), dma((2, 4)), dma((2,)),
    ]
    return pl.pallas_call(
        kernel,
        out_shape=jax.ShapeDtypeStruct((TOK, width), BF16),
        in_specs=[pl.BlockSpec(memory_space=pl.ANY)] * 5,
        out_specs=vmem,
        scratch_shapes=scratch,
        compiler_params=pltpu.CompilerParams(
            collective_id=0, has_side_effects=True, vmem_limit_bytes=56 * 2**20
        ),
    )(queries, keys, values, span_order, w_out)


def solution(mesh):
    return jax.shard_map(
        body,
        mesh=mesh,
        in_specs=(P("ctx", "grp"), P("ctx", None), P("ctx", None), P("ctx"), P("grp", None)),
        out_specs=P("ctx", "grp"),
        check_vma=False,
    )
```

time: 676 us -> 59.4 us (0.09)
  waiting for transfers between devices: 301 us -> 0 us
  local copies, waits for them, and re-layouts: 157 us -> 2.21 us
  matrix products: 143 us -> 0 us
  Pallas kernels: 0 us -> 56.8 us
  other arithmetic: 34.5 us -> 0 us
  blocking collectives: 22.7 us -> 0 us
  between operations: 13.9 us -> 0.01 us
    all_gather x2 -> x0, waiting for transfers between devices: 262 us -> none  [the longest x1 219 us: body(): lax.all_gather(values, 'ctx', axis=0, tiled=True)]
    gather x2 -> x0, local copies, waits for them, and re-layouts: 154 us -> none  [global_positions(): return order_table[row_ids // span] * span + row_ids % span]
    dot_general x97 -> x0, matrix products: 143 us -> none  [the longest x48 70.2 us: absorb(): jnp.einsum('hrc,cd->hrd', weights.astype(jnp.bfloat16), value_block, pref...]
    pallas_call x0 -> x1, Pallas kernels: none -> 56.8 us  [body(): pl.pallas_call(kernel, out_shape=jax.ShapeDtypeStruct((TOK, width), BF16)...]
    reduce_scatter x1 -> x0, waiting for transfers between devices: 37.1 us -> none  [body(): lax.psum_scatter(partial_term.astype(jnp.bfloat16), 'grp', scatter_dimens...]
    reduce_sum x48 -> x0, other arithmetic: 27.2 us -> none  [absorb(): denominator = denominator * fade_factor + jnp.sum(weights, axis=-1)]
    unnamed x1 -> x0, blocking collectives: 22.7 us -> none
  transfers between devices with their start and end apart: 3 -> 0, of which waited for: 3 -> 0; matrix products, arithmetic and copies ran while one was open for 23% -> 0% of each run, Pallas kernels for 0% -> 0%
where the time goes in v3:
time: 59.4 us; the launch traced here: 59 us
  Pallas kernels  56.8 us (96%)
  local copies, waits for them, and re-layouts  2.21 us (4%)
    pallas_call x1, Pallas kernels, body(): pl.pallas_call(kernel, out_shape=jax.ShapeDtypeStruct((TOK, width), BF16)...  56.8 us
    unnamed x1, local copies, waits for them, and re-layouts  2.21 us

profile of v3, /device:TPU:1, one launch (start us, length us, event | category | flops | bytes accessed | tf_op | source)
XLA Modules:
  0.0 59.0 jit_solution(1931353350485801538)
XLA Ops:
  0.0 56.8 %shard_map.55 = bf16[192,2560]{1,0:T(8,128)(2,1)} custom-call(bf16[192,512]{1,0:T(8,128)(2,1)} %q_hbm.1, bf16[192,128]{1,0:T(8,128)(2,1)} %k_hbm.1, bf16[192,128]{1,0:T(8,128)(2,1)} %v_hbm.1, s32[2]{0:T(128)} %order_hbm.1, bf16[512,5120]{1,0:T(8,128)(2,1)} %w_ref.1), custom_call_target="tpu_custom_call" | custom-call | tf_op jit(solution)/shard_map/pallas_call | solution.py:422
  56.8 2.2 %copy.7 = bf16[192,2560]{1,0:T(8,128)(2,1)} copy(bf16[192,2560]{1,0:T(8,128)(2,1)} %shard_map.55) | data formatting | bytes 1966080

commit v4 on v3

--- a/solution.py
+++ b/solution.py
@@ -80,33 +80,8 @@
             return pl.ds(group * COLS, COLS)
         return pl.ds(pl.multiple_of(group * COLS, COLS), COLS)
 
-    sub = iota((HD, COLS), 0)
-    col = iota((1, COLS), 1)
-    token = col % TOK
-    block = token // SPAN
-    step_row = token % SPAN + 8
-
-    @pl.loop(0, GROUPS)
-    def _(g):
-        far_y = jnp.logical_or(g // 2 == 1, g // 2 == 2)
-        hit = sub == block + 2 * (g % 2) + jnp.where(far_y, 4, 0)
-        same = jnp.logical_or(g == 0, g == GROUPS - 2)
-        hit = jnp.logical_or(hit, jnp.logical_and(sub == step_row, block == jnp.where(same, h, -1)))
-        qt[HD : 2 * HD, cols(g)] = jnp.where(hit, 1.0, 0.0).astype(BF16)
-
-    for k in range(CHUNKS):
-        vt[k, HD:VROWS, :] = jnp.ones((VROWS - HD, KEYS), BF16)
-
-    @pl.loop(0, TILES)
-    def _(t):
-        at = pl.ds(pl.multiple_of(t * TILE, TILE), TILE)
-        acc[:, at] = jnp.zeros((VROWS, TILE), F32)
-        mx[:, at] = jnp.full((8, TILE), -BIG, F32)
-
-    for copy in loads:
+    for copy in loads[:3]:
         copy.wait()
-    stacked = jnp.concatenate([q_ref[:, i * HD : (i + 1) * HD] for i in range(HEADS)], axis=0)
-    qt[0:HD, cols(0)] = stacked.T
     first, second = order_ref[0].astype(F32), order_ref[1].astype(F32)
     mine = jnp.where(h == 0, first, second)
     row0 = pl.multiple_of(h * SPAN, 16)
@@ -134,7 +109,12 @@
         q_on.append(
             remote(qt.at[0:HD, cols(2 * j)], qt.at[0:HD, cols(2 * j + 1)], q_s.at[3 + j], q_r.at[3 + j], device(dc=1))
         )
-    for copy in one_a + one_b + places + [q_core] + q_far[1:3]:
+    for copy in one_a + one_b + places:
+        copy.start()
+    loads[3].wait()
+    stacked = jnp.concatenate([q_ref[:, i * HD : (i + 1) * HD] for i in range(HEADS)], axis=0)
+    qt[0:HD, cols(0)] = stacked.T
+    for copy in [q_core] + q_far[1:3]:
         copy.start()
 
     o_half = pl.multiple_of((1 - h) * w_cols, 128)
@@ -263,6 +243,29 @@
         to = 3 * (j // 3) + (1 - j // 3) * (3 - j)
         start(*sum_copies(j, to, device(dy=turn)))
 
+    sub = iota((HD, COLS), 0)
+    col = iota((1, COLS), 1)
+    token = col % TOK
+    block = token // SPAN
+    step_row = token % SPAN + 8
+
+    @pl.loop(0, GROUPS)
+    def _(g):
+        far_y = jnp.logical_or(g // 2 == 1, g // 2 == 2)
+        hit = sub == block + 2 * (g % 2) + jnp.where(far_y, 4, 0)
+        same = jnp.logical_or(g == 0, g == GROUPS - 2)
+        hit = jnp.logical_or(hit, jnp.logical_and(sub == step_row, block == jnp.where(same, h, -1)))
+        qt[HD : 2 * HD, cols(g)] = jnp.where(hit, 1.0, 0.0).astype(BF16)
+
+    for k in range(CHUNKS):
+        vt[k, HD:VROWS, :] = jnp.ones((VROWS - HD, KEYS), BF16)
+
+    @pl.loop(0, TILES)
+    def _(t):
+        at = pl.ds(pl.multiple_of(t * TILE, TILE), TILE)
+        acc[:, at] = jnp.zeros((VROWS, TILE), F32)
+        mx[:, at] = jnp.full((8, TILE), -BIG, F32)
+
     receive(*one_a)
     start(q_far[3])
     assemble(bundle_a, stage_a, BLOCKS[0], SPLIT[0])
@@ -289,34 +292,23 @@
         if t == 5:
             receive(q_on[2], q_got[3])
             start(q_on[3])
-        if t == 9:
+        if t == 7:
             receive(q_on[3], ring[2], ring[3], ring[4], ring[5])
             start(ring[6], ring[7], ring[8], ring[9])
         if t == TILES - 1:
             prepare(1)
-        top = step((0, t), (0, t + 1) if t < TILES - 1 else (1, 0), t % 2, top)
-
-    def second(i, top):
-        base = i * 6
-        for t in range(6):
-            if t == 1:
-                @pl.when(i == 1)
-                def _():
-                    receive(ring[8], ring[9])
-                    start(ring[10], ring[11])
-            if t == 5:
-                @pl.when(i == 1)
-                def _():
-                    prepare(2)
-                    receive(w_cross)
-                    start(*w_x, w_on[0])
-                following = (jnp.where(i == 1, 2, 1), jnp.where(i == 1, TILES - 1, 6))
-            else:
-                following = (1, base + t + 1)
-            top = step((1, base + t), following, t % 2, top)
-        return top
-
-    top = lax.fori_loop(0, 2, second, top)
+        top = step((0, t), (0, t + 1) if t < TILES - 1 else (1, 3), t % 2, top)
+
+    for n, t in enumerate(range(3, TILES)):
+        if n == 7:
+            receive(w_cross)
+            start(*w_x, w_on[0])
+        if n == 4:
+            receive(ring[8], ring[9])
+            start(ring[10], ring[11])
+        if n == 8:
+            prepare(2)
+        top = step((1, t), (1, t + 1) if n < 8 else (2, TILES - 1), n % 2, top)
     receive(ring[6], ring[7], ring[10], ring[11])
     prepare(3)
 
@@ -329,22 +321,25 @@
                 pl.when(i > 0)(lambda: send_sum(j + 1))
             if n == 4:
                 hand_over(j)
-            following = (2 + (n + 1) % 2, base + 2 - (n + 1) // 2) if n < 5 else (2, base - 1)
-            top = step((k, t), following, n % 2, top)
+            following = (2 + (n + 1) % 2, base + 2 - (n + 1) // 2) if n < 5 else (jnp.where(i == 2, 1, 2), base - 1)
+            top = step((k, t), following, (n + 1) % 2, top)
         return top
 
     top = lax.fori_loop(0, 3, far, top)
-    for n in range(6):
-        k, t = 2 + n % 2, 2 - n // 2
+    last = [(k, t) for t in (2, 1, 0) for k in (1, 2, 3)]
+    for n, now in enumerate(last):
         if n == 2:
             send_sum(1)
-        if n == 4:
+        if n == 6:
             hand_over(0)
-        top = step((k, t), (2 + (n + 1) % 2, 2 - (n + 1) // 2) if n < 5 else None, n % 2, top)
+        if n == 7:
+            receive(*sum_copies(3, 3, device(dy=1)))
+            merge(0, p2_rx[3], s2_rx[3])
+        top = step(now, last[n + 1] if n < 8 else None, (n + 1) % 2, top)
 
     receive(*part_copies(0))
     merge(0, p1_rx[0], s1_rx[0])
-    for j in (3, 2, 1):
+    for j in (2, 1):
         receive(*sum_copies(j, j, device(dy=1)))
         merge(0, p2_rx[j], s2_rx[j])
     c_tx[...] = (acc[0:HD, cols(0)] / acc[HD : HD + 1, cols(0)]).astype(BF16)

time: 59.4 us -> 59.5 us (level)
  no operation moved by 1% of the time
where the time goes in v4:
time: 59.5 us; the launch traced here: 58.9 us
  Pallas kernels  56.7 us (95%)
  local copies, waits for them, and re-layouts  2.21 us (4%)
    pallas_call x1, Pallas kernels, body(): pl.pallas_call(kernel, out_shape=jax.ShapeDtypeStruct((TOK, width), BF16)...  56.7 us
    unnamed x1, local copies, waits for them, and re-layouts  2.21 us

profile of v4, /device:TPU:1, one launch (start us, length us, event | category | flops | bytes accessed | tf_op | source)
XLA Modules:
  0.0 58.9 jit_solution(823139900850113767)
XLA Ops:
  0.0 56.7 %shard_map.55 = bf16[192,2560]{1,0:T(8,128)(2,1)} custom-call(bf16[192,512]{1,0:T(8,128)(2,1)} %q_hbm.1, bf16[192,128]{1,0:T(8,128)(2,1)} %k_hbm.1, bf16[192,128]{1,0:T(8,128)(2,1)} %v_hbm.1, s32[2]{0:T(128)} %order_hbm.1, bf16[512,5120]{1,0:T(8,128)(2,1)} %w_ref.1), custom_call_target="tpu_custom_call" | custom-call | tf_op jit(solution)/shard_map/pallas_call | solution.py:417
  56.7 2.2 %copy.7 = bf16[192,2560]{1,0:T(8,128)(2,1)} copy(bf16[192,2560]{1,0:T(8,128)(2,1)} %shard_map.55) | data formatting | bytes 1966080
